TPU v7x, 512 devices: a whole 4x4x16 slice. The times are simulated.
512 devices in a mesh: nodes: 512 (over z, x, y, core).
Axes of the slice: x: 4, y: 4, z: 16, core: 2. Of those that a mesh axis runs over, the one named last changes fastest.
Arguments:
- tangent: float32 [2, 393216, 128], P(None, 'nodes'), as said below
- base_v: float32 [4, 393216], P(None, 'nodes'), may hold values from -2 to 2
- coupling: bfloat16 [1536, 8, 256, 256], P('nodes'), may hold values from -0.125 to 0.125
- columns: int32 [1536, 8], P('nodes'), may hold values from 0 to 1535, as said below
Outputs:
- basis: float32 [2, 393216, 128], P(None, 'nodes')
- growth: float32 [128, 128], replicated
Inputs may be any that keep to these rules, and one draw needn't show every extreme that they name: Block row r, held by index d = r // 3 of nodes, names 8 different block columns, all held by indices d - 1, d or d + 1 (cyclic over the axis). `tangent`: finite values.
All inputs are finite; a program needn't handle non-finite values.
Results may differ from a plain program's by a relative error of at most 0.00046.
Values may be sent and summed in bfloat16 or wider, within the bound.
A program may use at most 64 MiB of HBM per device.

v0:
```python
import jax
import jax.numpy as jnp
from jax import lax
from jax.sharding import PartitionSpec as P

STEPS = 4


time_step = 0.1
recovery_rate = 0.08
recovery_damp = 0.8


def with_halo(array, sides, width):
    for axis, dim in sides:
        size, length = (lax.axis_size(axis), array.shape[dim])
        up = [(i, (i + 1) % size) for i in range(size)]
        down = [(j, i) for i, j in up]
        last = lax.slice_in_dim(array, length - width, length, axis=dim)
        leading = lax.slice_in_dim(array, 0, width, axis=dim)
        before = lax.ppermute(last, axis, up)
        after = lax.ppermute(leading, axis, down)
        array = jnp.concatenate([before, array, after], axis=dim)
    return array


def from_partner(block, axis, apart):
    count = lax.axis_size(axis)
    route = []
    for low in range(count):
        high = low | 1 << apart
        if high != low and high < count:
            route += [(low, high), (high, low)]
    return lax.ppermute(block, axis, route)


def local(tangent, base_v, coupling, columns):
    blocks_here = coupling.shape[0]
    block_size = coupling.shape[2]
    vectors = tangent.shape[2]
    devices = lax.axis_size("nodes")
    first = lax.axis_index("nodes") * blocks_here
    total_blocks = blocks_here * devices
    relative = (columns - first + blocks_here) % total_blocks
    volt_rows = tangent[0]
    recov_rows = tangent[1]
    for section in range(STEPS):
        rounded = volt_rows.astype(jnp.bfloat16).reshape(blocks_here, block_size, vectors)
        extended = with_halo(rounded, (("nodes", 0),), blocks_here)
        chosen = extended[relative]
        coupled = jnp.einsum(
            "rkij,rkjc->ric", coupling, chosen, preferred_element_type=jnp.float32
        ).reshape(-1, vectors)
        volt = base_v[section][:, None]
        new_volt = volt_rows + time_step * ((1.0 - volt * volt) * volt_rows - recov_rows + coupled)
        new_recov = recov_rows + time_step * recovery_rate * (
            volt_rows - recovery_damp * recov_rows
        )
        volt_rows, recov_rows = (new_volt, new_recov)
    high = lax.Precision.HIGHEST
    local_gram = jnp.einsum("nk,nj->kj", volt_rows, volt_rows, precision=high) + jnp.einsum(
        "nk,nj->kj", recov_rows, recov_rows, precision=high
    )
    upper = jnp.linalg.cholesky(local_gram).T
    for level in range(devices.bit_length() - 1):
        partner = from_partner(upper, "nodes", level)
        joined = jnp.dot(upper.T, upper, precision=high) + jnp.dot(
            partner.T, partner, precision=high
        )
        upper = jnp.linalg.cholesky(joined).T
    lower = upper.T
    inverse = lax.linalg.triangular_solve(
        lower, jnp.eye(vectors, dtype=jnp.float32), left_side=True, lower=True
    )
    scale = jnp.sqrt(2.0 * total_blocks * block_size)
    basis = (
        jnp.stack(
            [
                jnp.dot(volt_rows, inverse.T, precision=high),
                jnp.dot(recov_rows, inverse.T, precision=high),
            ]
        )
        * scale
    )
    growth = lower.T / scale
    return (basis, growth)


def solution(mesh):
    placed = (
        P(None, "nodes", None),
        P(None, "nodes"),
        P("nodes", None, None, None),
        P("nodes", None),
    )
    return jax.shard_map(
        local, mesh=mesh, in_specs=placed, out_specs=(P(None, "nodes", None), P()), check_vma=False
    )
```

profile of v0, /device:TPU:2, one launch (start us, length us, event | category | flops | bytes accessed | tf_op | source)
XLA Modules:
  0.0 356.8 jit_solution(8042225786973514183)
XLA Ops:
  3.5 4.3 %collective-permute-start.1 = (bf16[3,256,128]{2,1,0:T(8,128)(2,1)}, bf16[3,256,128]{2,1,0:T(8,128)(2,1)}, u32[]{:S(2)}, u32[]{:S(2)}) collective-permute-start(bf16[3,256,128]{2,1,0:T(8,128)(2,1)} %convert_element_type.17), channel_id=1, source_target_pairs={{1,0},{2,1},{3,2},{4,3},{5,4},{6,5},{7,6},{8,7},{9,8},{10,9},{11,1... | collective-permute-start | bytes 589832 | tf_op jit(solution)/shard_map/ppermute | solution.py:22
  25.7 4.1 %collective-permute-start.3 = (bf16[3,256,128]{1,2,0:T(8,128)(2,1)}, bf16[3,256,128]{1,2,0:T(8,128)(2,1)}, u32[]{:S(2)}, u32[]{:S(2)}) collective-permute-start(bf16[3,256,128]{1,2,0:T(8,128)(2,1)} %get-tuple-element.22), channel_id=1, source_target_pairs={{1,0},{2,1},{3,2},{4,3},{5,4},{6,5},{7,6},{8,7},{9,8},{10,9},{11,1... | collective-permute-start | bytes 589832 | tf_op jit(solution)/shard_map/ppermute | solution.py:22
  33.3 5.9 %collective-permute-done.2 = bf16[3,256,128]{1,2,0:T(8,128)(2,1)} collective-permute-done((bf16[3,256,128]{1,2,0:T(8,128)(2,1)}, bf16[3,256,128]{1,2,0:T(8,128)(2,1)}, u32[]{:S(2)}, u32[]{:S(2)}) %collective-permute-start.2) | collective-permute-done | bytes 196640 | tf_op jit(solution)/shard_map/ppermute | solution.py:21
  44.2 3.6 %fusion.29 = (bf16[3,256,128]{1,2,0:T(8,128)(2,1)}, f32[3,256,128]{1,2,0:T(8,128)}) fusion(f32[3,256]{1,0:T(4,128)S(1)} %sub.164, f32[3,256,128]{1,2,0:T(8,128)} %copy.40, f32[3,256,128]{1,2,0:T(8,128)S(1)} %copy.41, f32[3,256,128]{1,2,0:T(8,128)} %get-tuple-element.23, f32[3,256]{1,0:T(4,128)S(1)} %sub.158, bf16[3,8,256,128]{2,3,1,0:T(8,128)(2,1)} %bitcast.239, ...), kind=kOutput, calls=%fused_computation.75 | convolution fusion | flops 404127744 | bytes 6494208 | tf_op jit(solution)/shard_map/rkij,rkjc->ric/dot_general | solution.py:51
  53.1 5.9 %collective-permute-done.4 = bf16[3,256,128]{1,2,0:T(8,128)(2,1)} collective-permute-done((bf16[3,256,128]{1,2,0:T(8,128)(2,1)}, bf16[3,256,128]{1,2,0:T(8,128)(2,1)}, u32[]{:S(2)}, u32[]{:S(2)}) %collective-permute-start.4) | collective-permute-done | bytes 196640 | tf_op jit(solution)/shard_map/ppermute | solution.py:21
  64.1 3.7 %add_convert_fusion = (bf16[3,256,128]{1,2,0:T(8,128)(2,1)}, f32[3,256,128]{1,2,0:T(8,128)}) fusion(f32[3,256,128]{1,2,0:T(8,128)} %get-tuple-element.25, f32[3,256]{1,0:T(4,128)S(1)} %sub.171, f32[3,256]{1,0:T(4,128)S(1)} %sub.164, f32[3,256,128]{1,2,0:T(8,128)} %copy.40, f32[3,256,128]{1,2,0:T(8,128)S(1)} %copy.41, f32[3,256,128]{1,2,0:T(8,128)} %get-tuple-element.23, ...), kind=kOutput, calls=%fused_computation.69 | convolution fusion | flops 405012480 | bytes 6890496 | tf_op jit(solution)/shard_map/rkij,rkjc->ric/dot_general | solution.py:51
  94.8 11.7 %cholesky.164 = f32[128,128]{1,0:T(8,128)S(1)} custom-call(f32[128,128]{1,0:T(8,128)S(1)} %fusion.45), custom_call_target="Cholesky" | custom-call | tf_op jit(solution)/shard_map/jit(cholesky)/cholesky | solution.py:64
  111.4 11.7 %cholesky.175 = f32[128,128]{1,0:T(8,128)S(1)} custom-call(f32[128,128]{1,0:T(8,128)S(1)} %fusion.44), custom_call_target="Cholesky" | custom-call | tf_op jit(solution)/shard_map/jit(cholesky)/cholesky | solution.py:70
  127.3 3.5 collective-permute-done.9
  131.1 11.7 %cholesky.186 = f32[128,128]{1,0:T(8,128)S(1)} custom-call(f32[128,128]{1,0:T(8,128)S(1)} %fusion.43), custom_call_target="Cholesky" | custom-call | tf_op jit(solution)/shard_map/jit(cholesky)/cholesky | solution.py:70
  152.2 11.7 %cholesky.197 = f32[128,128]{1,0:T(8,128)S(1)} custom-call(f32[128,128]{1,0:T(8,128)S(1)} %fusion.42), custom_call_target="Cholesky" | custom-call | tf_op jit(solution)/shard_map/jit(cholesky)/cholesky | solution.py:70
  165.3 26.9 %collective-permute-start.11 = (f32[128,128]{0,1:T(8,128)S(1)}, f32[128,128]{0,1:T(8,128)S(1)}, u32[]{:S(2)}, u32[]{:S(2)}) collective-permute-start(f32[128,128]{0,1:T(8,128)S(1)} %fusion.70), channel_id=1, source_target_pairs={{0,8},{8,0},{1,9},{9,1},{2,10},{10,2},{3,11},{11,3},{4,12},{12,4},... | collective-permute-start | bytes 196616 | tf_op jit(solution)/shard_map/ppermute | solution.py:34
  194.8 11.7 %cholesky.208 = f32[128,128]{1,0:T(8,128)S(1)} custom-call(f32[128,128]{1,0:T(8,128)S(1)} %fusion.41), custom_call_target="Cholesky" | custom-call | tf_op jit(solution)/shard_map/jit(cholesky)/cholesky | solution.py:70
  211.1 4.4 %collective-permute-done.12 = f32[128,128]{0,1:T(8,128)S(1)} collective-permute-done((f32[128,128]{0,1:T(8,128)S(1)}, f32[128,128]{0,1:T(8,128)S(1)}, u32[]{:S(2)}, u32[]{:S(2)}) %collective-permute-start.12) | collective-permute-done | bytes 65568 | tf_op jit(solution)/shard_map/ppermute | solution.py:34
  215.9 11.7 %cholesky.219 = f32[128,128]{1,0:T(8,128)S(1)} custom-call(f32[128,128]{1,0:T(8,128)S(1)} %fusion.40), custom_call_target="Cholesky" | custom-call | tf_op jit(solution)/shard_map/jit(cholesky)/cholesky | solution.py:70
  235.5 11.7 %cholesky.230 = f32[128,128]{1,0:T(8,128)S(1)} custom-call(f32[128,128]{1,0:T(8,128)S(1)} %fusion.39), custom_call_target="Cholesky" | custom-call | tf_op jit(solution)/shard_map/jit(cholesky)/cholesky | solution.py:70
  251.6 4.2 %collective-permute-done.14 = f32[128,128]{0,1:T(8,128)S(1)} collective-permute-done((f32[128,128]{0,1:T(8,128)S(1)}, f32[128,128]{0,1:T(8,128)S(1)}, u32[]{:S(2)}, u32[]{:S(2)}) %collective-permute-start.14) | collective-permute-done | bytes 65568 | tf_op jit(solution)/shard_map/ppermute | solution.py:34
  256.1 11.7 %cholesky.241 = f32[128,128]{1,0:T(8,128)S(1)} custom-call(f32[128,128]{1,0:T(8,128)S(1)} %fusion.38), custom_call_target="Cholesky" | custom-call | tf_op jit(solution)/shard_map/jit(cholesky)/cholesky | solution.py:70
  274.5 7.2 %collective-permute-done.15 = f32[128,128]{0,1:T(8,128)S(1)} collective-permute-done((f32[128,128]{0,1:T(8,128)S(1)}, f32[128,128]{0,1:T(8,128)S(1)}, u32[]{:S(2)}, u32[]{:S(2)}) %collective-permute-start.15) | collective-permute-done | bytes 65568 | tf_op jit(solution)/shard_map/ppermute | solution.py:34
  285.6 13.2 %cholesky.252 = f32[128,128]{1,0:T(8,128)} custom-call(f32[128,128]{1,0:T(8,128)} %fusion.37), custom_call_target="Cholesky" | custom-call | tf_op jit(solution)/shard_map/jit(cholesky)/cholesky | solution.py:70
  301.8 6.6 %collective-permute-start.16 = (f32[128,128]{0,1:T(8,128)S(1)}, f32[128,128]{0,1:T(8,128)S(1)}, u32[]{:S(2)}, u32[]{:S(2)}) collective-permute-start(f32[128,128]{0,1:T(8,128)S(1)} %fusion.80), channel_id=1, source_target_pairs={{0,256},{256,0},{1,257},{257,1},{2,258},{258,2},{3,259},{259,3},{4... | collective-permute-start | bytes 196616 | tf_op jit(solution)/shard_map/ppermute | solution.py:34
  310.2 7.0 %collective-permute-done.16 = f32[128,128]{0,1:T(8,128)S(1)} collective-permute-done((f32[128,128]{0,1:T(8,128)S(1)}, f32[128,128]{0,1:T(8,128)S(1)}, u32[]{:S(2)}, u32[]{:S(2)}) %collective-permute-start.16) | collective-permute-done | bytes 65568 | tf_op jit(solution)/shard_map/ppermute | solution.py:34
  321.2 13.2 %cholesky.263 = f32[128,128]{1,0:T(8,128)} custom-call(f32[128,128]{1,0:T(8,128)} %fusion.36), custom_call_target="Cholesky" | custom-call | tf_op jit(solution)/shard_map/jit(cholesky)/cholesky | solution.py:70
  338.1 11.3 %custom-call.5 = f32[1,128,128]{1,2,0:T(8,128)} custom-call(f32[1,128,128]{2,1,0:T(8,128)} %get-tuple-element.21), custom_call_target="InvertDiagBlocksLowerTriangular" | custom-call | tf_op jit(solution)/shard_map/triangular_solve | solution.py:72
  (155 shorter events, 136.9 us)
Async XLA Ops:
  0.6 21.6 %copy-start = (bf16[3,8,256,256]{3,2,1,0:T(8,128)(2,1)S(1)}, bf16[3,8,256,256]{3,2,1,0:T(8,128)(2,1)}, u32[]{:S(2)}) copy-start(bf16[3,8,256,256]{3,2,1,0:T(8,128)(2,1)} %param.7) | copy-start | bytes 9437188
  0.6 12.2 %copy-start.14 = (s32[3,8]{1,0:T(4,128)S(1)}, s32[3,8]{1,0:T(4,128)}, u32[]{:S(2)}) copy-start(s32[3,8]{1,0:T(4,128)} %param.8) | copy-start | bytes 292
  3.5 12.1 %collective-permute-start.1 = (bf16[3,256,128]{2,1,0:T(8,128)(2,1)}, bf16[3,256,128]{2,1,0:T(8,128)(2,1)}, u32[]{:S(2)}, u32[]{:S(2)}) collective-permute-start(bf16[3,256,128]{2,1,0:T(8,128)(2,1)} %convert_element_type.17), channel_id=1, source_target_pairs={{1,0},{2,1},{3,2},{4,3},{5,4},{6,5},{7,6},{8,7},{9,8},{10,9},{11,1... | collective-permute-start | bytes 589832 | tf_op jit(solution)/shard_map/ppermute | solution.py:22
  7.8 9.4 %collective-permute-start = (bf16[3,256,128]{2,1,0:T(8,128)(2,1)}, bf16[3,256,128]{2,1,0:T(8,128)(2,1)}, u32[]{:S(2)}, u32[]{:S(2)}) collective-permute-start(bf16[3,256,128]{2,1,0:T(8,128)(2,1)} %convert_element_type.17), channel_id=1, source_target_pairs={{0,1},{1,2},{2,3},{3,4},{4,5},{5,6},{6,7},{7,8},{8,9},{9,10},{10,1... | collective-permute-start | bytes 589832 | tf_op jit(solution)/shard_map/ppermute | solution.py:21
  14.3 7.9 %copy-start.8 = (f32[768]{0:T(1024)}, f32[768]{0:T(1024)S(1)}, u32[]{:S(2)}) copy-start(f32[768]{0:T(1024)S(1)} %get-tuple-element.9) | copy-start | bytes 9220
  15.6 25.7 %copy-start.12 = (s32[1024]{0:T(1024)}, s32[1024]{0:T(1024)S(1)}, u32[]{:S(2)}) copy-start(s32[1024]{0:T(1024)S(1)} %pad_clamp_fusion) | copy-start | bytes 12292
  25.7 7.6 %collective-permute-start.3 = (bf16[3,256,128]{1,2,0:T(8,128)(2,1)}, bf16[3,256,128]{1,2,0:T(8,128)(2,1)}, u32[]{:S(2)}, u32[]{:S(2)}) collective-permute-start(bf16[3,256,128]{1,2,0:T(8,128)(2,1)} %get-tuple-element.22), channel_id=1, source_target_pairs={{1,0},{2,1},{3,2},{4,3},{5,4},{6,5},{7,6},{8,7},{9,8},{10,9},{11,1... | collective-permute-start | bytes 589832 | tf_op jit(solution)/shard_map/ppermute | solution.py:22
  29.8 9.4 %collective-permute-start.2 = (bf16[3,256,128]{1,2,0:T(8,128)(2,1)}, bf16[3,256,128]{1,2,0:T(8,128)(2,1)}, u32[]{:S(2)}, u32[]{:S(2)}) collective-permute-start(bf16[3,256,128]{1,2,0:T(8,128)(2,1)} %get-tuple-element.22), channel_id=1, source_target_pairs={{0,1},{1,2},{2,3},{3,4},{4,5},{5,6},{6,7},{7,8},{8,9},{9,10},{10,1... | collective-permute-start | bytes 589832 | tf_op jit(solution)/shard_map/ppermute | solution.py:21
  47.7 5.4 %collective-permute-start.5 = (bf16[3,256,128]{1,2,0:T(8,128)(2,1)}, bf16[3,256,128]{1,2,0:T(8,128)(2,1)}, u32[]{:S(2)}, u32[]{:S(2)}) collective-permute-start(bf16[3,256,128]{1,2,0:T(8,128)(2,1)} %get-tuple-element.24), channel_id=1, source_target_pairs={{1,0},{2,1},{3,2},{4,3},{5,4},{6,5},{7,6},{8,7},{9,8},{10,9},{11,1... | collective-permute-start | bytes 589832 | tf_op jit(solution)/shard_map/ppermute | solution.py:22
  49.6 9.4 %collective-permute-start.4 = (bf16[3,256,128]{1,2,0:T(8,128)(2,1)}, bf16[3,256,128]{1,2,0:T(8,128)(2,1)}, u32[]{:S(2)}, u32[]{:S(2)}) collective-permute-start(bf16[3,256,128]{1,2,0:T(8,128)(2,1)} %get-tuple-element.24), channel_id=1, source_target_pairs={{0,1},{1,2},{2,3},{3,4},{4,5},{5,6},{6,7},{7,8},{8,9},{9,10},{10,1... | collective-permute-start | bytes 589832 | tf_op jit(solution)/shard_map/ppermute | solution.py:21
  67.8 9.5 %collective-permute-start.7 = (bf16[3,256,128]{1,2,0:T(8,128)(2,1)}, bf16[3,256,128]{1,2,0:T(8,128)(2,1)}, u32[]{:S(2)}, u32[]{:S(2)}) collective-permute-start(bf16[3,256,128]{1,2,0:T(8,128)(2,1)} %get-tuple-element.26), channel_id=1, source_target_pairs={{1,0},{2,1},{3,2},{4,3},{5,4},{6,5},{7,6},{8,7},{9,8},{10,9},{11,1... | collective-permute-start | bytes 589832 | tf_op jit(solution)/shard_map/ppermute | solution.py:22
  69.7 9.4 %collective-permute-start.6 = (bf16[3,256,128]{1,2,0:T(8,128)(2,1)}, bf16[3,256,128]{1,2,0:T(8,128)(2,1)}, u32[]{:S(2)}, u32[]{:S(2)}) collective-permute-start(bf16[3,256,128]{1,2,0:T(8,128)(2,1)} %get-tuple-element.26), channel_id=1, source_target_pairs={{0,1},{1,2},{2,3},{3,4},{4,5},{5,6},{6,7},{7,8},{8,9},{9,10},{10,1... | collective-permute-start | bytes 589832 | tf_op jit(solution)/shard_map/ppermute | solution.py:21
  73.4 7.7 %copy-start.13 = (s32[1024]{0:T(1024)S(1)}, s32[1024]{0:T(1024)}, u32[]{:S(2)}) copy-start(s32[1024]{0:T(1024)} %copy-done.12) | copy-start | bytes 12292
  84.0 5.2 %copy-start.11 = (f32[768]{0:T(1024)S(1)}, f32[768]{0:T(1024)}, u32[]{:S(2)}) copy-start(f32[768]{0:T(1024)} %get-tuple-element.7) | copy-start | bytes 9220
  107.8 3.1 collective-permute-start.8
  124.4 6.3 %collective-permute-start.9 = (f32[128,128]{0,1:T(8,128)S(1)}, f32[128,128]{0,1:T(8,128)S(1)}, u32[]{:S(2)}, u32[]{:S(2)}) collective-permute-start(f32[128,128]{0,1:T(8,128)S(1)} %fusion.66), channel_id=1, source_target_pairs={{0,2},{2,0},{1,3},{3,1},{4,6},{6,4},{5,7},{7,5},{8,10},{10,8},{9,1... | collective-permute-start | bytes 196616 | tf_op jit(solution)/shard_map/ppermute | solution.py:34
  144.2 7.7 %collective-permute-start.10 = (f32[128,128]{0,1:T(8,128)S(1)}, f32[128,128]{0,1:T(8,128)S(1)}, u32[]{:S(2)}, u32[]{:S(2)}) collective-permute-start(f32[128,128]{0,1:T(8,128)S(1)} %fusion.68), channel_id=1, source_target_pairs={{0,4},{4,0},{1,5},{5,1},{2,6},{6,2},{3,7},{7,3},{8,12},{12,8},{9,1... | collective-permute-start | bytes 196616 | tf_op jit(solution)/shard_map/ppermute | solution.py:34
  165.3 29.1 %collective-permute-start.11 = (f32[128,128]{0,1:T(8,128)S(1)}, f32[128,128]{0,1:T(8,128)S(1)}, u32[]{:S(2)}, u32[]{:S(2)}) collective-permute-start(f32[128,128]{0,1:T(8,128)S(1)} %fusion.70), channel_id=1, source_target_pairs={{0,8},{8,0},{1,9},{9,1},{2,10},{10,2},{3,11},{11,3},{4,12},{12,4},... | collective-permute-start | bytes 196616 | tf_op jit(solution)/shard_map/ppermute | solution.py:34
  207.8 7.7 %collective-permute-start.12 = (f32[128,128]{0,1:T(8,128)S(1)}, f32[128,128]{0,1:T(8,128)S(1)}, u32[]{:S(2)}, u32[]{:S(2)}) collective-permute-start(f32[128,128]{0,1:T(8,128)S(1)} %fusion.72), channel_id=1, source_target_pairs={{0,16},{16,0},{1,17},{17,1},{2,18},{18,2},{3,19},{19,3},{4,20},{20... | collective-permute-start | bytes 196616 | tf_op jit(solution)/shard_map/ppermute | solution.py:34
  228.9 6.2 %collective-permute-start.13 = (f32[128,128]{0,1:T(8,128)S(1)}, f32[128,128]{0,1:T(8,128)S(1)}, u32[]{:S(2)}, u32[]{:S(2)}) collective-permute-start(f32[128,128]{0,1:T(8,128)S(1)} %fusion.74), channel_id=1, source_target_pairs={{0,32},{32,0},{1,33},{33,1},{2,34},{34,2},{3,35},{35,3},{4,36},{36... | collective-permute-start | bytes 196616 | tf_op jit(solution)/shard_map/ppermute | solution.py:34
  248.5 7.2 %collective-permute-start.14 = (f32[128,128]{0,1:T(8,128)S(1)}, f32[128,128]{0,1:T(8,128)S(1)}, u32[]{:S(2)}, u32[]{:S(2)}) collective-permute-start(f32[128,128]{0,1:T(8,128)S(1)} %fusion.76), channel_id=1, source_target_pairs={{0,64},{64,0},{1,65},{65,1},{2,66},{66,2},{3,67},{67,3},{4,68},{68... | collective-permute-start | bytes 196616 | tf_op jit(solution)/shard_map/ppermute | solution.py:34
  269.2 84.9 %copy-start.6 = (f32[768,128]{1,0:T(8,128)S(1)}, f32[768,128]{1,0:T(8,128)}, u32[]{:S(2)}) copy-start(f32[768,128]{1,0:T(8,128)} %get-tuple-element.12) | copy-start | bytes 1179652
  270.7 10.9 %collective-permute-start.15 = (f32[128,128]{0,1:T(8,128)S(1)}, f32[128,128]{0,1:T(8,128)S(1)}, u32[]{:S(2)}, u32[]{:S(2)}) collective-permute-start(f32[128,128]{0,1:T(8,128)S(1)} %fusion.78), channel_id=1, source_target_pairs={{0,128},{128,0},{1,129},{129,1},{2,130},{130,2},{3,131},{131,3},{4... | collective-permute-start | bytes 196616 | tf_op jit(solution)/shard_map/ppermute | solution.py:34
  301.8 15.4 %collective-permute-start.16 = (f32[128,128]{0,1:T(8,128)S(1)}, f32[128,128]{0,1:T(8,128)S(1)}, u32[]{:S(2)}, u32[]{:S(2)}) collective-permute-start(f32[128,128]{0,1:T(8,128)S(1)} %fusion.80), channel_id=1, source_target_pairs={{0,256},{256,0},{1,257},{257,1},{2,258},{258,2},{3,259},{259,3},{4... | collective-permute-start | bytes 196616 | tf_op jit(solution)/shard_map/ppermute | solution.py:34
  (8 other events, 28.7 us)
where the time goes:
time: 363 us; the launch traced here: 357 us
  other arithmetic  168 us (46%)
  starting transfers between devices  70.3 us (19%)
  waiting for transfers between devices  51.5 us (14%)
  matrix products  34.1 us (9%)
  local copies, waits for them, and re-layouts  31.3 us (9%)
    another operation x27, other arithmetic, local(): upper = jnp.linalg.cholesky(joined).T  116 us
    ppermute x9, starting transfers between devices, from_partner(): return lax.ppermute(block, axis, route)  49.2 us
    ppermute x9, waiting for transfers between devices, from_partner(): return lax.ppermute(block, axis, route)  34.3 us
    ppermute x4, waiting for transfers between devices, with_halo(): before = lax.ppermute(last, axis, up)  15.3 us
    dot_general x4, matrix products, local(): jnp.einsum('rkij,rkjc->ric', coupling, chosen, preferred_element_type=jnp...  14 us
    another operation x3, other arithmetic, local(): upper = jnp.linalg.cholesky(local_gram).T  12.4 us
    ppermute x4, starting transfers between devices, with_halo(): after = lax.ppermute(leading, axis, down)  12.3 us
    gather x4, local copies, waits for them, and re-layouts, local(): chosen = extended[relative]  11.9 us
  transfers between devices with their start and end apart: 17, of which 15 were waited for; matrix products, arithmetic and copies ran while one was open for 6% of the time, Pallas kernels for 0%

commit v1 on v0

v1 whole, which is shorter than its diff:
```python
import functools

import jax
import jax.numpy as jnp
from jax import lax
from jax.experimental import pallas as pl
from jax.experimental.pallas import tpu as pltpu
from jax.sharding import PartitionSpec as P

STEPS = 4
MESH = pl.DeviceIdType.MESH
HIGH = lax.Precision.HIGHEST

time_step = 0.1
recovery_rate = 0.08
recovery_damp = 0.8


def tangent_kernel(
    devices, plane, tan_ref, v_ref, coup_ref, col_ref, state_ref, gram_ref,
    tv, tw, acc, coef, raw, weights, own, before, after, parts, got, zbuf, total,
    load_sem, send_sem, recv_sem, red_send, red_recv, out_sem,
):
    blocks, links, size, _ = coup_ref.shape
    rows, vectors = tv.shape
    count = 3 * blocks
    tall = devices // plane
    piece = vectors // plane
    me = lax.axis_index("nodes")
    level, place = me // plane, me % plane
    right, left = (me + 1) % devices, (me + devices - 1) % devices

    def plane_peer(k):
        return level * plane + (place + k) % plane

    def tall_peer(k):
        return ((level + k) % tall) * plane + place

    barrier = pltpu.get_barrier_semaphore()

    def greet(device):
        pl.semaphore_signal(barrier, inc=1, device_id=(device,), device_id_type=MESH)

    greet(left)
    greet(right)

    @pl.loop(1, plane)
    def _(k):
        greet(plane_peer(k))

    @pl.loop(1, tall)
    def _(k):
        greet(tall_peer(k))

    load = pltpu.make_async_copy(coup_ref, raw.at[pl.ds(0, blocks)], load_sem)
    load.start()
    raw[blocks, 0] = jnp.zeros((size, size), jnp.bfloat16)
    for b in range(blocks):
        span = pl.ds(b * size, size)
        own[0, span, :] = tan_ref[0, span, :].astype(jnp.bfloat16)
    pl.semaphore_wait(barrier, 2 + (plane - 1) + (tall - 1))

    def sends(step, b):
        span = pl.ds(b * size, size)
        return [
            pltpu.make_async_remote_copy(
                src_ref=own.at[step, span, :],
                dst_ref=dst.at[step, span, :],
                send_sem=send_sem.at[step, side, b],
                recv_sem=recv_sem.at[step, side, b],
                device_id=(target,),
                device_id_type=MESH,
            )
            for side, (dst, target) in enumerate(((before, right), (after, left)))
        ]

    for b in range(blocks):
        for copy in sends(0, b):
            copy.start()

    first = me * blocks
    names = [[(col_ref[r, k] - first + blocks * (devices + 1)) % (blocks * devices) for k in range(links)] for r in range(blocks)]
    volt = v_ref[...]
    factor = 1.0 + time_step * (1.0 - volt * volt)
    factor = jnp.concatenate([factor, factor], axis=0).T
    for s in range(STEPS):
        coef[s] = jnp.broadcast_to(factor[:, s : s + 1], (rows, vectors))
    load.wait()
    for r in range(blocks):
        for c in range(count):
            at_r, at_k = blocks, 0
            for k in range(links):
                hit = names[r][k] == c
                at_r = jnp.where(hit, r, at_r)
                at_k = jnp.where(hit, k, at_k)
            weights[pl.ds(r * size, size), pl.ds(c * size, size)] = raw[at_r, at_k]

    def product(row_span, c, value):
        return jnp.dot(
            weights[row_span, pl.ds(c * size, size)], value, preferred_element_type=jnp.float32
        )

    everything = pl.ds(0, rows)
    gram_w = None
    for s in range(STEPS):
        old_v = tan_ref[0] if s == 0 else tv[...]
        old_w = tan_ref[1] if s == 0 else tw[...]
        acc[...] = old_v * coef[s] - time_step * old_w
        tw[...] = old_w + time_step * recovery_rate * (old_v - recovery_damp * old_w)
        acc[...] += time_step * jnp.dot(
            weights[:, pl.ds(blocks * size, blocks * size)], own[s], preferred_element_type=jnp.float32
        )
        if s == STEPS - 1:
            last_w = tw[...]
            gram_w = lax.dot_general(
                last_w, last_w, (((0,), (0,)), ((), ())), precision=HIGH, preferred_element_type=jnp.float32
            )
            store_w = pltpu.make_async_copy(tw, state_ref.at[1], out_sem.at[1])
            store_w.start()
        for b in range(blocks):
            arrived = sends(s, b)
            span = pl.ds(b * size, size)
            arrived[0].wait_recv()
            arrived[1].wait_recv()
            if b < blocks - 1:
                acc[...] += time_step * (
                    product(everything, b, before[s, span, :])
                    + product(everything, 2 * blocks + b, after[s, span, :])
                )
        last = pl.ds((blocks - 1) * size, size)
        for r in range(blocks):
            span = pl.ds(r * size, size)
            new = acc[span, :] + time_step * (
                product(span, blocks - 1, before[s, last, :]) + product(span, count - 1, after[s, last, :])
            )
            tv[span, :] = new
            if s < STEPS - 1:
                own[s + 1, span, :] = new.astype(jnp.bfloat16)
                for copy in sends(s + 1, r):
                    copy.start()

    store_v = pltpu.make_async_copy(tv, state_ref.at[0], out_sem.at[0])
    store_v.start()
    last_v = tv[...]
    local = gram_w + lax.dot_general(
        last_v, last_v, (((0,), (0,)), ((), ())), precision=HIGH, preferred_element_type=jnp.float32
    )
    for i in range(plane):
        parts[i] = local[i * piece : (i + 1) * piece, :]

    def spread(phase, src, dst, target):
        return pltpu.make_async_remote_copy(
            src_ref=src,
            dst_ref=dst,
            send_sem=red_send.at[phase],
            recv_sem=red_recv.at[phase],
            device_id=(target,),
            device_id_type=MESH,
        )

    def all_of(phase, ref, slots):
        span = ref.at[pl.ds(0, slots)]
        return spread(phase, span, span, right)

    @pl.loop(1, plane)
    def _(k):
        peer = (place + k) % plane
        spread(0, parts.at[peer], got.at[k - 1], plane_peer(k)).start()

    all_of(0, got, plane - 1).wait_recv()
    mine = parts[place] + jnp.sum(got[...], axis=0)
    zbuf[level] = mine

    @pl.loop(1, tall)
    def _(k):
        spread(1, zbuf.at[level], zbuf.at[level], tall_peer(k)).start()

    all_of(1, zbuf, tall - 1).wait_recv()
    total[place] = jnp.sum(zbuf[...], axis=0)

    @pl.loop(1, plane)
    def _(k):
        spread(2, total.at[place], total.at[place], plane_peer(k)).start()

    all_of(2, total, plane - 1).wait_recv()
    for i in range(plane):
        gram_ref[i * piece : (i + 1) * piece, :] = total[i]

    for s in range(STEPS):
        for b in range(blocks):
            for copy in sends(s, b):
                copy.wait_send()
    all_of(0, got, plane - 1).wait_send()
    all_of(1, zbuf, tall - 1).wait_send()
    all_of(2, total, plane - 1).wait_send()
    store_w.wait()
    store_v.wait()


def factor_rows(gram, width):
    lane = lax.broadcasted_iota(jnp.int32, (8, width), 1)
    sub = lax.broadcasted_iota(jnp.int32, (8, width), 0)
    wide = lambda x: jnp.broadcast_to(x, (8, width))
    panels = [gram[8 * q : 8 * q + 8, :] for q in range(width // 8)]
    upper, inverse = [], []
    for p in range(width // 8):
        panel = panels[p]
        base = 8 * p
        cols = [wide(panel[:, base + k : base + k + 1]) for k in range(8)]
        diag = {(s, k): wide(cols[k][s : s + 1, :]) for k in range(8) for s in range(k, 8)}
        in_block = (lane >= base) & (lane < base + 8)
        mixed = jnp.where(in_block, jnp.where(lane - base == sub, 1.0, 0.0), panel)
        row_a = [wide(panel[s : s + 1, :]) for s in range(8)]
        row_c = [wide(mixed[s : s + 1, :]) for s in range(8)]
        inv = []
        for i in range(8):
            inv.append(lax.rsqrt(diag[i, i]))
            row_a[i] = row_a[i] * inv[i]
            row_c[i] = row_c[i] * inv[i]
            for s in range(i + 1, 8):
                diag[s, i] = diag[s, i] * inv[i]
            for s in range(i + 1, 8):
                for k in range(i + 1, s + 1):
                    diag[s, k] = diag[s, k] - diag[s, i] * diag[k, i]
                row_a[s] = row_a[s] - diag[s, i] * row_a[i]
                row_c[s] = row_c[s] - diag[s, i] * row_c[i]
        out_a, out_c = row_a[7], row_c[7]
        for s in range(7):
            out_a = jnp.where(sub == s, row_a[s], out_a)
            out_c = jnp.where(sub == s, row_c[s], out_c)
        upper.append(jnp.where(lane >= base + sub, out_a, 0.0))
        inverse.append(jnp.where(lane <= base + sub, out_c, 0.0))
        back = [None] * 8
        for i in range(7, -1, -1):
            value = row_c[i]
            for s in range(i + 1, 8):
                value = value - diag[s, i] * back[s]
            back[i] = value * inv[i]
        for q in range(p + 1, width // 8):
            value = jnp.where(in_block, 0.0, panels[q])
            for k in range(8):
                value = value - wide(panels[q][:, base + k : base + k + 1]) * back[k]
            panels[q] = value
    return upper, inverse


def basis_kernel(scale, gram_ref, state_ref, basis_ref, growth_ref, state, inverse, out, in_sem, out_sem):
    vectors = gram_ref.shape[0]
    load = pltpu.make_async_copy(state_ref, state, in_sem)
    load.start()
    upper, low = factor_rows(gram_ref[...], vectors)
    for p, (a, c) in enumerate(zip(upper, low)):
        growth_ref[8 * p : 8 * p + 8, :] = a * (1.0 / scale)
        inverse[8 * p : 8 * p + 8, :] = c * scale
    load.wait()
    for half in range(2):
        out[half] = lax.dot_general(
            state[half], inverse[...], (((1,), (1,)), ((), ())), precision=HIGH, preferred_element_type=jnp.float32
        )
        pltpu.make_async_copy(out.at[half], basis_ref.at[half], out_sem.at[half]).start()
    for half in range(2):
        pltpu.make_async_copy(out.at[half], basis_ref.at[half], out_sem.at[half]).wait()


def local(tangent, base_v, coupling, columns, *, plane=32):
    blocks, links, size, _ = coupling.shape
    _, rows, vectors = tangent.shape
    devices = lax.axis_size("nodes")
    count = 3 * blocks
    tall, piece = devices // plane, vectors // plane
    vmem = pl.BlockSpec(memory_space=pltpu.VMEM)
    anywhere = pl.BlockSpec(memory_space=pl.ANY)
    f32, bf16 = jnp.float32, jnp.bfloat16
    dma = pltpu.SemaphoreType.DMA
    state, gram = pl.pallas_call(
        functools.partial(tangent_kernel, devices, plane),
        out_shape=(
            jax.ShapeDtypeStruct((2, rows, vectors), f32),
            jax.ShapeDtypeStruct((vectors, vectors), f32),
        ),
        in_specs=[vmem, vmem, anywhere, pl.BlockSpec(memory_space=pltpu.SMEM)],
        out_specs=(anywhere, vmem),
        scratch_shapes=[
            pltpu.VMEM((rows, vectors), f32),
            pltpu.VMEM((rows, vectors), f32),
            pltpu.VMEM((rows, vectors), f32),
            pltpu.VMEM((STEPS, rows, vectors), f32),
            pltpu.VMEM((blocks + 1, links, size, size), bf16),
            pltpu.VMEM((rows, count * size), bf16),
            pltpu.VMEM((STEPS, rows, vectors), bf16),
            pltpu.VMEM((STEPS, rows, vectors), bf16),
            pltpu.VMEM((STEPS, rows, vectors), bf16),
            pltpu.VMEM((plane, piece, vectors), f32),
            pltpu.VMEM((plane - 1, piece, vectors), f32),
            pltpu.VMEM((tall, piece, vectors), f32),
            pltpu.VMEM((plane, piece, vectors), f32),
            dma,
            dma((STEPS, 2, blocks)),
            dma((STEPS, 2, blocks)),
            dma((3,)),
            dma((3,)),
            dma((2,)),
        ],
        compiler_params=pltpu.CompilerParams(
            collective_id=0, has_side_effects=True, vmem_limit_bytes=40 * 2**20
        ),
    )(tangent, base_v, coupling, columns)
    scale = float((2.0 * rows * devices) ** 0.5)
    return pl.pallas_call(
        functools.partial(basis_kernel, scale),
        out_shape=(
            jax.ShapeDtypeStruct((2, rows, vectors), f32),
            jax.ShapeDtypeStruct((vectors, vectors), f32),
        ),
        in_specs=[vmem, anywhere],
        out_specs=(anywhere, vmem),
        scratch_shapes=[
            pltpu.VMEM((2, rows, vectors), f32),
            pltpu.VMEM((vectors, vectors), f32),
            pltpu.VMEM((2, rows, vectors), f32),
            dma,
            dma((2,)),
        ],
        compiler_params=pltpu.CompilerParams(vmem_limit_bytes=40 * 2**20),
    )(gram, state)


def solution(mesh):
    placed = (
        P(None, "nodes", None),
        P(None, "nodes"),
        P("nodes", None, None, None),
        P("nodes", None),
    )
    return jax.shard_map(
        local, mesh=mesh, in_specs=placed, out_specs=(P(None, "nodes", None), P()), check_vma=False
    )
```

time: 363 us -> 77.5 us (0.21)
  the two profiles are of different devices: /device:TPU:2 before, /device:TPU:1 now
where the time goes in v1:
time: 77.5 us; the launch traced here: 77.3 us
  Pallas kernels  72.2 us (93%)
  local copies, waits for them, and re-layouts  4.4 us (6%)
    pallas_call x1, Pallas kernels, local(): pl.pallas_call(functools.partial(tangent_kernel, devices, plane), out_sha...  64.4 us
    pallas_call x1, Pallas kernels, local(): pl.pallas_call(functools.partial(basis_kernel, scale), out_shape=(jax.Sha...  7.79 us
    unnamed x8, local copies, waits for them, and re-layouts  4.4 us

profile of v1, /device:TPU:1, one launch (start us, length us, event | category | flops | bytes accessed | tf_op | source)
XLA Modules:
  0.0 77.3 jit_solution(15023336247746208026)
XLA Ops:
  0.6 0.0 copy-start
  0.6 1.9 %copy-done = bf16[3,8,256,256]{3,2,1,0:T(8,128)(2,1)S(1)} copy-done((bf16[3,8,256,256]{3,2,1,0:T(8,128)(2,1)S(1)}, bf16[3,8,256,256]{3,2,1,0:T(8,128)(2,1)}, u32[]{:S(2)}) %copy-start) | copy-done | bytes 3145752
  2.5 0.0 copy-start.1
  2.5 1.1 %copy-done.1 = f32[2,768,128]{2,1,0:T(8,128)S(1)} copy-done((f32[2,768,128]{2,1,0:T(8,128)S(1)}, f32[2,768,128]{2,1,0:T(8,128)}, u32[]{:S(2)}) %copy-start.1) | copy-done | bytes 786456
  3.7 0.0 copy-start.2
  3.7 0.7 copy-done.2
  4.4 0.0 copy-start.3
  4.4 0.7 copy-done.3
  5.0 64.4 %shard_map.59 = (f32[2,768,128]{2,1,0:T(8,128)S(1)}, f32[128,128]{1,0:T(8,128)S(1)}) custom-call(f32[2,768,128]{2,1,0:T(8,128)S(1)} %copy-done.1, f32[4,768]{1,0:T(4,128)S(1)} %copy-done.2, bf16[3,8,256,256]{3,2,1,0:T(8,128)(2,1)S(1)} %copy-done, s32[3,8]{1,0:T(4,128)S(1)} %copy-done.3), custom_call_target="tpu_custom_call" | custom-call | tf_op jit(solution)/shard_map/pallas_call | solution.py:275
  69.5 7.8 %shard_map.60 = (f32[2,768,128]{2,1,0:T(8,128)}, f32[128,128]{1,0:T(8,128)}) custom-call(f32[128,128]{1,0:T(8,128)S(1)} %get-tuple-element.4.gram_ref, f32[2,768,128]{2,1,0:T(8,128)S(1)} %get-tuple-element.5.state_ref), custom_call_target="tpu_custom_call" | custom-call | tf_op jit(solution)/shard_map/pallas_call | solution.py:309
Async XLA Ops:
  0.6 1.9 %copy-start = (bf16[3,8,256,256]{3,2,1,0:T(8,128)(2,1)S(1)}, bf16[3,8,256,256]{3,2,1,0:T(8,128)(2,1)}, u32[]{:S(2)}) copy-start(bf16[3,8,256,256]{3,2,1,0:T(8,128)(2,1)} %coup_ref.1) | copy-start | bytes 9437188
  2.5 1.1 %copy-start.1 = (f32[2,768,128]{2,1,0:T(8,128)S(1)}, f32[2,768,128]{2,1,0:T(8,128)}, u32[]{:S(2)}) copy-start(f32[2,768,128]{2,1,0:T(8,128)} %tan_ref.1) | copy-start | bytes 2359300
  3.7 0.7 copy-start.2
  4.4 0.7 copy-start.3

commit v2 on v1

--- a/solution.py
+++ b/solution.py
@@ -17,47 +17,65 @@
 
 
 def tangent_kernel(
-    devices, plane, tan_ref, v_ref, coup_ref, col_ref, state_ref, gram_ref,
-    tv, tw, acc, coef, raw, weights, own, before, after, parts, got, zbuf, total,
+    devices, grid, tan_ref, v_hbm, coup_ref, col_hbm, state_ref, gram_ref,
+    v_ref, col_ref, tv, tw, acc, coef, raw, weights, own, before, after, parts, got, zbuf, total,
     load_sem, send_sem, recv_sem, red_send, red_recv, out_sem,
 ):
     blocks, links, size, _ = coup_ref.shape
     rows, vectors = tv.shape
     count = 3 * blocks
+    plane = grid[0] * grid[1] * grid[2]
     tall = devices // plane
     piece = vectors // plane
     me = lax.axis_index("nodes")
     level, place = me // plane, me % plane
     right, left = (me + 1) % devices, (me + devices - 1) % devices
 
-    def plane_peer(k):
-        return level * plane + (place + k) % plane
-
-    def tall_peer(k):
-        return ((level + k) % tall) * plane + place
-
+    around = lambda shift, size: min(shift, size - shift)
+    shifts = sorted(
+        ((a, b, c) for a in range(grid[0]) for b in range(grid[1]) for c in range(grid[2]) if a + b + c > 0),
+        key=lambda t: -(4 * around(t[0], grid[0]) + 4 * around(t[1], grid[1]) + t[2]),
+    )
+    at_a, at_b, at_c = place // (grid[1] * grid[2]), place // grid[2] % grid[1], place % grid[2]
+    plane_peers = [
+        ((at_a + a) % grid[0] * grid[1] + (at_b + b) % grid[1]) * grid[2] + (at_c + c) % grid[2]
+        for a, b, c in shifts
+    ]
+    tall_peers = [
+        (level + k) % tall * plane + place for k in sorted(range(1, tall), key=lambda k: -around(k, tall))
+    ]
+
+    loads = [
+        pltpu.make_async_copy(src, dst, load_sem.at[i])
+        for i, (src, dst) in enumerate(
+            (
+                (tan_ref.at[0], tv),
+                (col_hbm, col_ref),
+                (v_hbm, v_ref),
+                (coup_ref, raw.at[pl.ds(0, blocks)]),
+                (tan_ref.at[1], tw),
+            )
+        )
+    ]
+    loads[0].start()
     barrier = pltpu.get_barrier_semaphore()
 
     def greet(device):
         pl.semaphore_signal(barrier, inc=1, device_id=(device,), device_id_type=MESH)
 
+    for peer in tall_peers:
+        greet(peer)
+    for peer in plane_peers:
+        greet(level * plane + peer)
     greet(left)
     greet(right)
-
-    @pl.loop(1, plane)
-    def _(k):
-        greet(plane_peer(k))
-
-    @pl.loop(1, tall)
-    def _(k):
-        greet(tall_peer(k))
-
-    load = pltpu.make_async_copy(coup_ref, raw.at[pl.ds(0, blocks)], load_sem)
-    load.start()
+    for load in loads[1:]:
+        load.start()
     raw[blocks, 0] = jnp.zeros((size, size), jnp.bfloat16)
+    loads[0].wait()
     for b in range(blocks):
         span = pl.ds(b * size, size)
-        own[0, span, :] = tan_ref[0, span, :].astype(jnp.bfloat16)
+        own[0, span, :] = tv[span, :].astype(jnp.bfloat16)
     pl.semaphore_wait(barrier, 2 + (plane - 1) + (tall - 1))
 
     def sends(step, b):
@@ -78,14 +96,16 @@
         for copy in sends(0, b):
             copy.start()
 
+    loads[1].wait()
     first = me * blocks
     names = [[(col_ref[r, k] - first + blocks * (devices + 1)) % (blocks * devices) for k in range(links)] for r in range(blocks)]
+    loads[2].wait()
     volt = v_ref[...]
     factor = 1.0 + time_step * (1.0 - volt * volt)
     factor = jnp.concatenate([factor, factor], axis=0).T
     for s in range(STEPS):
         coef[s] = jnp.broadcast_to(factor[:, s : s + 1], (rows, vectors))
-    load.wait()
+    loads[3].wait()
     for r in range(blocks):
         for c in range(count):
             at_r, at_k = blocks, 0
@@ -100,11 +120,11 @@
             weights[row_span, pl.ds(c * size, size)], value, preferred_element_type=jnp.float32
         )
 
+    loads[4].wait()
     everything = pl.ds(0, rows)
     gram_w = None
     for s in range(STEPS):
-        old_v = tan_ref[0] if s == 0 else tv[...]
-        old_w = tan_ref[1] if s == 0 else tw[...]
+        old_v, old_w = tv[...], tw[...]
         acc[...] = old_v * coef[s] - time_step * old_w
         tw[...] = old_w + time_step * recovery_rate * (old_v - recovery_damp * old_w)
         acc[...] += time_step * jnp.dot(
@@ -162,25 +182,21 @@
         span = ref.at[pl.ds(0, slots)]
         return spread(phase, span, span, right)
 
-    @pl.loop(1, plane)
-    def _(k):
-        peer = (place + k) % plane
-        spread(0, parts.at[peer], got.at[k - 1], plane_peer(k)).start()
+    for k, peer in enumerate(plane_peers):
+        spread(0, parts.at[peer], got.at[k], level * plane + peer).start()
 
     all_of(0, got, plane - 1).wait_recv()
     mine = parts[place] + jnp.sum(got[...], axis=0)
     zbuf[level] = mine
 
-    @pl.loop(1, tall)
-    def _(k):
-        spread(1, zbuf.at[level], zbuf.at[level], tall_peer(k)).start()
+    for peer in tall_peers:
+        spread(1, zbuf.at[level], zbuf.at[level], peer).start()
 
     all_of(1, zbuf, tall - 1).wait_recv()
     total[place] = jnp.sum(zbuf[...], axis=0)
 
-    @pl.loop(1, plane)
-    def _(k):
-        spread(2, total.at[place], total.at[place], plane_peer(k)).start()
+    for peer in plane_peers:
+        spread(2, total.at[place], total.at[place], level * plane + peer).start()
 
     all_of(2, total, plane - 1).wait_recv()
     for i in range(plane):
@@ -201,9 +217,10 @@
     lane = lax.broadcasted_iota(jnp.int32, (8, width), 1)
     sub = lax.broadcasted_iota(jnp.int32, (8, width), 0)
     wide = lambda x: jnp.broadcast_to(x, (8, width))
-    panels = [gram[8 * q : 8 * q + 8, :] for q in range(width // 8)]
+    count = width // 8
+    panels = [gram[8 * q : 8 * q + 8, :] for q in range(count)]
     upper, inverse = [], []
-    for p in range(width // 8):
+    for p in range(count):
         panel = panels[p]
         base = 8 * p
         cols = [wide(panel[:, base + k : base + k + 1]) for k in range(8)]
@@ -212,11 +229,14 @@
         mixed = jnp.where(in_block, jnp.where(lane - base == sub, 1.0, 0.0), panel)
         row_a = [wide(panel[s : s + 1, :]) for s in range(8)]
         row_c = [wide(mixed[s : s + 1, :]) for s in range(8)]
+        nxt = [wide(panels[p + 1][:, base + k : base + k + 1]) for k in range(8)] if p + 1 < count else None
+        nval = jnp.where(in_block, 0.0, panels[p + 1]) if p + 1 < count else None
         inv = []
         for i in range(8):
             inv.append(lax.rsqrt(diag[i, i]))
             row_a[i] = row_a[i] * inv[i]
             row_c[i] = row_c[i] * inv[i]
+            if nxt: nxt[i] = nxt[i] * inv[i]
             for s in range(i + 1, 8):
                 diag[s, i] = diag[s, i] * inv[i]
             for s in range(i + 1, 8):
@@ -224,19 +244,23 @@
                     diag[s, k] = diag[s, k] - diag[s, i] * diag[k, i]
                 row_a[s] = row_a[s] - diag[s, i] * row_a[i]
                 row_c[s] = row_c[s] - diag[s, i] * row_c[i]
+                if nxt: nxt[s] = nxt[s] - diag[s, i] * nxt[i]
+            if nxt: nval = nval - nxt[i] * row_c[i]
         out_a, out_c = row_a[7], row_c[7]
         for s in range(7):
             out_a = jnp.where(sub == s, row_a[s], out_a)
             out_c = jnp.where(sub == s, row_c[s], out_c)
         upper.append(jnp.where(lane >= base + sub, out_a, 0.0))
         inverse.append(jnp.where(lane <= base + sub, out_c, 0.0))
+        if nxt:
+            panels[p + 1] = nval
         back = [None] * 8
         for i in range(7, -1, -1):
             value = row_c[i]
             for s in range(i + 1, 8):
                 value = value - diag[s, i] * back[s]
             back[i] = value * inv[i]
-        for q in range(p + 1, width // 8):
+        for q in range(p + 2, count):
             value = jnp.where(in_block, 0.0, panels[q])
             for k in range(8):
                 value = value - wide(panels[q][:, base + k : base + k + 1]) * back[k]
@@ -262,25 +286,28 @@
         pltpu.make_async_copy(out.at[half], basis_ref.at[half], out_sem.at[half]).wait()
 
 
-def local(tangent, base_v, coupling, columns, *, plane=32):
+def local(tangent, base_v, coupling, columns, *, grid=(4, 4, 2)):
     blocks, links, size, _ = coupling.shape
     _, rows, vectors = tangent.shape
     devices = lax.axis_size("nodes")
     count = 3 * blocks
+    plane = grid[0] * grid[1] * grid[2]
     tall, piece = devices // plane, vectors // plane
     vmem = pl.BlockSpec(memory_space=pltpu.VMEM)
     anywhere = pl.BlockSpec(memory_space=pl.ANY)
     f32, bf16 = jnp.float32, jnp.bfloat16
     dma = pltpu.SemaphoreType.DMA
     state, gram = pl.pallas_call(
-        functools.partial(tangent_kernel, devices, plane),
+        functools.partial(tangent_kernel, devices, grid),
         out_shape=(
             jax.ShapeDtypeStruct((2, rows, vectors), f32),
             jax.ShapeDtypeStruct((vectors, vectors), f32),
         ),
-        in_specs=[vmem, vmem, anywhere, pl.BlockSpec(memory_space=pltpu.SMEM)],
+        in_specs=[pl.BlockSpec(memory_space=pltpu.HBM)] * 4,
         out_specs=(anywhere, vmem),
         scratch_shapes=[
+            pltpu.VMEM((STEPS, rows), f32),
+            pltpu.SMEM((blocks, links), jnp.int32),
             pltpu.VMEM((rows, vectors), f32),
             pltpu.VMEM((rows, vectors), f32),
             pltpu.VMEM((rows, vectors), f32),
@@ -294,7 +321,7 @@
             pltpu.VMEM((plane - 1, piece, vectors), f32),
             pltpu.VMEM((tall, piece, vectors), f32),
             pltpu.VMEM((plane, piece, vectors), f32),
-            dma,
+            dma((5,)),
             dma((STEPS, 2, blocks)),
             dma((STEPS, 2, blocks)),
             dma((3,)),
@@ -304,7 +331,7 @@
         compiler_params=pltpu.CompilerParams(
             collective_id=0, has_side_effects=True, vmem_limit_bytes=40 * 2**20
         ),
-    )(tangent, base_v, coupling, columns)
+    )(*(pltpu.with_memory_space_constraint(x, pltpu.HBM) for x in (tangent, base_v, coupling, columns)))
     scale = float((2.0 * rows * devices) ** 0.5)
     return pl.pallas_call(
         functools.partial(basis_kernel, scale),

time: 77.5 us -> 70.8 us (0.914)
  local copies, waits for them, and re-layouts: 4.4 us -> 0 us
  Pallas kernels: 72.2 us -> 69.9 us
    unnamed x8 -> x0, local copies, waits for them, and re-layouts: 4.4 us -> none
    pallas_call x1, Pallas kernels: 64.4 us -> 63.2 us  [local(): pl.pallas_call(functools.partial(tangent_kernel, devices, grid), out_shap...]
    pallas_call x1, Pallas kernels: 7.79 us -> 6.66 us  [local(): pl.pallas_call(functools.partial(basis_kernel, scale), out_shape=(jax.Sha...]
where the time goes in v2:
time: 70.8 us; the launch traced here: 70.7 us
  Pallas kernels  69.9 us (99%)
  between operations  0.8 us (1%)
    pallas_call x1, Pallas kernels, local(): pl.pallas_call(functools.partial(tangent_kernel, devices, grid), out_shap...  63.2 us
    pallas_call x1, Pallas kernels, local(): pl.pallas_call(functools.partial(basis_kernel, scale), out_shape=(jax.Sha...  6.66 us

profile of v2, /device:TPU:1, one launch (start us, length us, event | category | flops | bytes accessed | tf_op | source)
XLA Modules:
  0.0 70.7 jit_solution(5337851112396284688)
XLA Ops:
  0.6 63.2 %shard_map.59 = (f32[2,768,128]{2,1,0:T(8,128)S(1)}, f32[128,128]{1,0:T(8,128)S(1)}) custom-call(f32[2,768,128]{2,1,0:T(8,128)} %tan_ref.1, f32[4,768]{1,0:T(4,128)} %v_hbm.1, bf16[3,8,256,256]{3,2,1,0:T(8,128)(2,1)} %coup_ref.1, s32[3,8]{1,0:T(4,128)} %col_hbm.1), custom_call_target="tpu_custom_call" | custom-call | tf_op jit(solution)/shard_map/pallas_call | solution.py:300
  63.9 6.7 %shard_map.60 = (f32[2,768,128]{2,1,0:T(8,128)}, f32[128,128]{1,0:T(8,128)}) custom-call(f32[128,128]{1,0:T(8,128)S(1)} %get-tuple-element.4.gram_ref, f32[2,768,128]{2,1,0:T(8,128)S(1)} %get-tuple-element.5.state_ref), custom_call_target="tpu_custom_call" | custom-call | tf_op jit(solution)/shard_map/pallas_call | solution.py:336

commit v3 on v2

--- a/solution.py
+++ b/solution.py
@@ -8,6 +8,7 @@
 from jax.sharding import PartitionSpec as P
 
 STEPS = 4
+GROUPS = 2
 MESH = pl.DeviceIdType.MESH
 HIGH = lax.Precision.HIGHEST
 
@@ -18,18 +19,22 @@
 
 def tangent_kernel(
     devices, grid, tan_ref, v_hbm, coup_ref, col_hbm, state_ref, gram_ref,
-    v_ref, col_ref, tv, tw, acc, coef, raw, weights, own, before, after, parts, got, zbuf, total,
+    v_ref, col_ref, full, sv, sw, acc, coef, raw, weights, own, near, far, parts, got, zbuf, total,
     load_sem, send_sem, recv_sem, red_send, red_recv, out_sem,
 ):
     blocks, links, size, _ = coup_ref.shape
-    rows, vectors = tv.shape
+    _, rows, vectors = full.shape
+    half, lanes = size // 2, vectors // 2
+    packed = rows // 2
     count = 3 * blocks
     plane = grid[0] * grid[1] * grid[2]
     tall = devices // plane
     piece = vectors // plane
     me = lax.axis_index("nodes")
     level, place = me // plane, me % plane
-    right, left = (me + 1) % devices, (me + devices - 1) % devices
+    odd = me % 2
+    partner = me + 1 - 2 * odd
+    other = (me + devices - 1 + 2 * odd) % devices
 
     around = lambda shift, size: min(shift, size - shift)
     shifts = sorted(
@@ -49,11 +54,11 @@
         pltpu.make_async_copy(src, dst, load_sem.at[i])
         for i, (src, dst) in enumerate(
             (
-                (tan_ref.at[0], tv),
+                (tan_ref.at[0], full.at[0]),
                 (col_hbm, col_ref),
                 (v_hbm, v_ref),
                 (coup_ref, raw.at[pl.ds(0, blocks)]),
-                (tan_ref.at[1], tw),
+                (tan_ref.at[1], full.at[1]),
             )
         )
     ]
@@ -67,34 +72,56 @@
         greet(peer)
     for peer in plane_peers:
         greet(level * plane + peer)
-    greet(left)
-    greet(right)
+    greet(other)
+    greet(partner)
     for load in loads[1:]:
         load.start()
     raw[blocks, 0] = jnp.zeros((size, size), jnp.bfloat16)
+    low = lax.broadcasted_iota(jnp.int32, (half, vectors), 1) < lanes
+
+    def turn(x):
+        return pltpu.roll(x, lanes, axis=1)
+
+    def pack(which, store):
+        for b in range(blocks):
+            top = full[which, pl.ds(b * size, half), :]
+            bottom = full[which, pl.ds(b * size + half, half), :]
+            store(0, b, jnp.where(low, top, turn(bottom)))
+            store(1, b, jnp.where(low, turn(top), bottom))
+
+    def unpack(which, group):
+        for b in range(blocks):
+            zero, one = group[0, pl.ds(b * half, half), :], group[1, pl.ds(b * half, half), :]
+            full[which, pl.ds(b * size, half), :] = jnp.where(low, zero, turn(one))
+            full[which, pl.ds(b * size + half, half), :] = jnp.where(low, turn(zero), one)
+
+    def start_voltage(g, b, value):
+        sv[g, pl.ds(b * half, half), :] = value
+        own[0, g, pl.ds(b * half, half), :] = value.astype(jnp.bfloat16)
+
+    def start_recovery(g, b, value):
+        sw[g, pl.ds(b * half, half), :] = value
+
     loads[0].wait()
-    for b in range(blocks):
-        span = pl.ds(b * size, size)
-        own[0, span, :] = tv[span, :].astype(jnp.bfloat16)
+    pack(0, start_voltage)
     pl.semaphore_wait(barrier, 2 + (plane - 1) + (tall - 1))
 
-    def sends(step, b):
-        span = pl.ds(b * size, size)
-        return [
-            pltpu.make_async_remote_copy(
-                src_ref=own.at[step, span, :],
-                dst_ref=dst.at[step, span, :],
-                send_sem=send_sem.at[step, side, b],
-                recv_sem=recv_sem.at[step, side, b],
-                device_id=(target,),
-                device_id_type=MESH,
-            )
-            for side, (dst, target) in enumerate(((before, right), (after, left)))
-        ]
-
-    for b in range(blocks):
-        for copy in sends(0, b):
-            copy.start()
+    def send(step, g, b, side):
+        span = pl.ds(b * half, half)
+        dst, target = ((near, partner), (far, other))[side]
+        return pltpu.make_async_remote_copy(
+            src_ref=own.at[step, g, span, :],
+            dst_ref=dst.at[step, g, span, :],
+            send_sem=send_sem.at[step, g, side, b],
+            recv_sem=recv_sem.at[step, g, side, b],
+            device_id=(target,),
+            device_id_type=MESH,
+        )
+
+    for g in range(GROUPS):
+        for b in range(blocks):
+            send(0, g, b, 1).start()
+            send(0, g, b, 0).start()
 
     loads[1].wait()
     first = me * blocks
@@ -104,67 +131,90 @@
     factor = 1.0 + time_step * (1.0 - volt * volt)
     factor = jnp.concatenate([factor, factor], axis=0).T
     for s in range(STEPS):
-        coef[s] = jnp.broadcast_to(factor[:, s : s + 1], (rows, vectors))
+        for b in range(blocks):
+            top, bottom = (
+                jnp.broadcast_to(factor[b * size + at : b * size + at + half, s : s + 1], (half, vectors))
+                for at in (0, half)
+            )
+            coef[s, pl.ds(b * half, half), :] = jnp.where(low, top, bottom)
     loads[3].wait()
+    starts = (blocks, 2 * blocks * (1 - odd), 2 * blocks * odd)
     for r in range(blocks):
         for c in range(count):
             at_r, at_k = blocks, 0
             for k in range(links):
-                hit = names[r][k] == c
+                hit = names[r][k] == starts[c // blocks] + c % blocks
                 at_r = jnp.where(hit, r, at_r)
                 at_k = jnp.where(hit, k, at_k)
-            weights[pl.ds(r * size, size), pl.ds(c * size, size)] = raw[at_r, at_k]
-
-    def product(row_span, c, value):
+            block = raw[at_r, at_k]
+            weights[pl.ds(r * size, half), pl.ds(c * size, size)] = block[:half]
+            for side in range(2):
+                weights[pl.ds(r * size + half, half), pl.ds(c * size + side * half, half)] = block[
+                    half:, (1 - side) * half : (2 - side) * half
+                ]
+
+    def both(*values):
+        return jnp.concatenate([y for x in values for y in (x, turn(x))], axis=0)
+
+    def product(row_span, at, operand):
         return jnp.dot(
-            weights[row_span, pl.ds(c * size, size)], value, preferred_element_type=jnp.float32
+            weights[row_span, pl.ds(at * size, operand.shape[0])], operand, preferred_element_type=jnp.float32
+        )
+
+    def own_part(s, g):
+        old_v, old_w = sv[g], sw[g]
+        sv[g] = old_v * coef[s] - time_step * old_w
+        sw[g] = old_w + time_step * recovery_rate * (old_v - recovery_damp * old_w)
+        operand = both(*(own[s, g, pl.ds(b * half, half), :] for b in range(blocks)))
+        acc[g] = product(pl.ds(0, rows), 0, operand)
+
+    def near_part(s, g):
+        for b in range(blocks):
+            send(s, g, b, 0).wait_recv()
+        operand = both(*(near[s, g, pl.ds(b * half, half), :] for b in range(blocks)))
+        acc[g] += product(pl.ds(0, rows), blocks, operand)
+
+    def finish(s, g):
+        for b in range(blocks):
+            send(s, g, b, 1).wait_recv()
+        operand = both(*(far[s, g, pl.ds(b * half, half), :] for b in range(blocks)))
+        for r in range(blocks):
+            span = pl.ds(r * half, half)
+            here = pl.ds(r * size, size)
+            coupled = acc[g, here, :] + product(here, 2 * blocks, operand)
+            new = sv[g, span, :] + time_step * jnp.where(low, coupled[:half], coupled[half:])
+            sv[g, span, :] = new
+            if s < STEPS - 1:
+                own[s + 1, g, span, :] = new.astype(jnp.bfloat16)
+                send(s + 1, g, r, 1).start()
+                send(s + 1, g, r, 0).start()
+
+    def gram_of(which):
+        x = full[which]
+        return lax.dot_general(
+            x, x, (((0,), (0,)), ((), ())), precision=HIGH, preferred_element_type=jnp.float32
         )
 
     loads[4].wait()
-    everything = pl.ds(0, rows)
-    gram_w = None
+    pack(1, start_recovery)
+    for g in range(GROUPS):
+        own_part(0, g)
     for s in range(STEPS):
-        old_v, old_w = tv[...], tw[...]
-        acc[...] = old_v * coef[s] - time_step * old_w
-        tw[...] = old_w + time_step * recovery_rate * (old_v - recovery_damp * old_w)
-        acc[...] += time_step * jnp.dot(
-            weights[:, pl.ds(blocks * size, blocks * size)], own[s], preferred_element_type=jnp.float32
-        )
-        if s == STEPS - 1:
-            last_w = tw[...]
-            gram_w = lax.dot_general(
-                last_w, last_w, (((0,), (0,)), ((), ())), precision=HIGH, preferred_element_type=jnp.float32
-            )
-            store_w = pltpu.make_async_copy(tw, state_ref.at[1], out_sem.at[1])
+        for g in range(GROUPS):
+            near_part(s, g)
+        for g in range(GROUPS):
+            finish(s, g)
+            if s < STEPS - 1:
+                own_part(s + 1, g)
+        if s == STEPS - 2:
+            unpack(1, sw)
+            store_w = pltpu.make_async_copy(full.at[1], state_ref.at[1], out_sem.at[1])
             store_w.start()
-        for b in range(blocks):
-            arrived = sends(s, b)
-            span = pl.ds(b * size, size)
-            arrived[0].wait_recv()
-            arrived[1].wait_recv()
-            if b < blocks - 1:
-                acc[...] += time_step * (
-                    product(everything, b, before[s, span, :])
-                    + product(everything, 2 * blocks + b, after[s, span, :])
-                )
-        last = pl.ds((blocks - 1) * size, size)
-        for r in range(blocks):
-            span = pl.ds(r * size, size)
-            new = acc[span, :] + time_step * (
-                product(span, blocks - 1, before[s, last, :]) + product(span, count - 1, after[s, last, :])
-            )
-            tv[span, :] = new
-            if s < STEPS - 1:
-                own[s + 1, span, :] = new.astype(jnp.bfloat16)
-                for copy in sends(s + 1, r):
-                    copy.start()
-
-    store_v = pltpu.make_async_copy(tv, state_ref.at[0], out_sem.at[0])
+            gram_w = gram_of(1)
+    unpack(0, sv)
+    store_v = pltpu.make_async_copy(full.at[0], state_ref.at[0], out_sem.at[0])
     store_v.start()
-    last_v = tv[...]
-    local = gram_w + lax.dot_general(
-        last_v, last_v, (((0,), (0,)), ((), ())), precision=HIGH, preferred_element_type=jnp.float32
-    )
+    local = gram_w + gram_of(0)
     for i in range(plane):
         parts[i] = local[i * piece : (i + 1) * piece, :]
 
@@ -180,7 +230,7 @@
 
     def all_of(phase, ref, slots):
         span = ref.at[pl.ds(0, slots)]
-        return spread(phase, span, span, right)
+        return spread(phase, span, span, partner)
 
     for k, peer in enumerate(plane_peers):
         spread(0, parts.at[peer], got.at[k], level * plane + peer).start()
@@ -203,9 +253,10 @@
         gram_ref[i * piece : (i + 1) * piece, :] = total[i]
 
     for s in range(STEPS):
-        for b in range(blocks):
-            for copy in sends(s, b):
-                copy.wait_send()
+        for g in range(GROUPS):
+            for b in range(blocks):
+                for side in range(2):
+                    send(s, g, b, side).wait_send()
     all_of(0, got, plane - 1).wait_send()
     all_of(1, zbuf, tall - 1).wait_send()
     all_of(2, total, plane - 1).wait_send()
@@ -308,22 +359,23 @@
         scratch_shapes=[
             pltpu.VMEM((STEPS, rows), f32),
             pltpu.SMEM((blocks, links), jnp.int32),
-            pltpu.VMEM((rows, vectors), f32),
-            pltpu.VMEM((rows, vectors), f32),
-            pltpu.VMEM((rows, vectors), f32),
-            pltpu.VMEM((STEPS, rows, vectors), f32),
+            pltpu.VMEM((2, rows, vectors), f32),
+            pltpu.VMEM((GROUPS, rows // 2, vectors), f32),
+            pltpu.VMEM((GROUPS, rows // 2, vectors), f32),
+            pltpu.VMEM((GROUPS, rows, vectors), f32),
+            pltpu.VMEM((STEPS, rows // 2, vectors), f32),
             pltpu.VMEM((blocks + 1, links, size, size), bf16),
             pltpu.VMEM((rows, count * size), bf16),
-            pltpu.VMEM((STEPS, rows, vectors), bf16),
-            pltpu.VMEM((STEPS, rows, vectors), bf16),
-            pltpu.VMEM((STEPS, rows, vectors), bf16),
+            pltpu.VMEM((STEPS, GROUPS, rows // 2, vectors), bf16),
+            pltpu.VMEM((STEPS, GROUPS, rows // 2, vectors), bf16),
+            pltpu.VMEM((STEPS, GROUPS, rows // 2, vectors), bf16),
             pltpu.VMEM((plane, piece, vectors), f32),
             pltpu.VMEM((plane - 1, piece, vectors), f32),
             pltpu.VMEM((tall, piece, vectors), f32),
             pltpu.VMEM((plane, piece, vectors), f32),
             dma((5,)),
-            dma((STEPS, 2, blocks)),
-            dma((STEPS, 2, blocks)),
+            dma((STEPS, GROUPS, 2, blocks)),
+            dma((STEPS, GROUPS, 2, blocks)),
             dma((3,)),
             dma((3,)),
             dma((2,)),

time: 70.8 us -> 69 us (0.975)
  Pallas kernels: 69.9 us -> 68.1 us
    pallas_call x1, Pallas kernels: 63.2 us -> 61.4 us  [local(): pl.pallas_call(functools.partial(tangent_kernel, devices, grid), out_shap...]
where the time goes in v3:
time: 69 us; the launch traced here: 68.9 us
  Pallas kernels  68.1 us (99%)
  between operations  0.8 us (1%)
    pallas_call x1, Pallas kernels, local(): pl.pallas_call(functools.partial(tangent_kernel, devices, grid), out_shap...  61.4 us
    pallas_call x1, Pallas kernels, local(): pl.pallas_call(functools.partial(basis_kernel, scale), out_shape=(jax.Sha...  6.66 us

profile of v3, /device:TPU:1, one launch (start us, length us, event | category | flops | bytes accessed | tf_op | source)
XLA Modules:
  0.0 68.9 jit_solution(14567587219648082007)
XLA Ops:
  0.6 61.4 %shard_map.59 = (f32[2,768,128]{2,1,0:T(8,128)S(1)}, f32[128,128]{1,0:T(8,128)S(1)}) custom-call(f32[2,768,128]{2,1,0:T(8,128)} %tan_ref.1, f32[4,768]{1,0:T(4,128)} %v_hbm.1, bf16[3,8,256,256]{3,2,1,0:T(8,128)(2,1)} %coup_ref.1, s32[3,8]{1,0:T(4,128)} %col_hbm.1), custom_call_target="tpu_custom_call" | custom-call | tf_op jit(solution)/shard_map/pallas_call | solution.py:351
  62.1 6.7 %shard_map.60 = (f32[2,768,128]{2,1,0:T(8,128)}, f32[128,128]{1,0:T(8,128)}) custom-call(f32[128,128]{1,0:T(8,128)S(1)} %get-tuple-element.4.gram_ref, f32[2,768,128]{2,1,0:T(8,128)S(1)} %get-tuple-element.5.state_ref), custom_call_target="tpu_custom_call" | custom-call | tf_op jit(solution)/shard_map/pallas_call | solution.py:388

commit v4 on v3

--- a/solution.py
+++ b/solution.py
@@ -9,6 +9,7 @@
 
 STEPS = 4
 GROUPS = 2
+PIECES = 3
 MESH = pl.DeviceIdType.MESH
 HIGH = lax.Precision.HIGHEST
 
@@ -242,29 +243,29 @@
     for peer in tall_peers:
         spread(1, zbuf.at[level], zbuf.at[level], peer).start()
 
-    all_of(1, zbuf, tall - 1).wait_recv()
-    total[place] = jnp.sum(zbuf[...], axis=0)
-
-    for peer in plane_peers:
-        spread(2, total.at[place], total.at[place], level * plane + peer).start()
-
-    all_of(2, total, plane - 1).wait_recv()
-    for i in range(plane):
-        gram_ref[i * piece : (i + 1) * piece, :] = total[i]
-
     for s in range(STEPS):
         for g in range(GROUPS):
             for b in range(blocks):
                 for side in range(2):
                     send(s, g, b, side).wait_send()
     all_of(0, got, plane - 1).wait_send()
-    all_of(1, zbuf, tall - 1).wait_send()
-    all_of(2, total, plane - 1).wait_send()
     store_w.wait()
     store_v.wait()
-
-
-def factor_rows(gram, width):
+    all_of(1, zbuf, tall - 1).wait_recv()
+    total[place] = jnp.sum(zbuf[...], axis=0)
+
+    for peer in plane_peers:
+        spread(2, total.at[place], total.at[place], level * plane + peer).start()
+
+    all_of(1, zbuf, tall - 1).wait_send()
+    all_of(2, total, plane - 1).wait_recv()
+    for i in range(plane):
+        gram_ref[i * piece : (i + 1) * piece, :] = total[i]
+
+    all_of(2, total, plane - 1).wait_send()
+
+
+def factor_rows(gram, width, scratch):
     lane = lax.broadcasted_iota(jnp.int32, (8, width), 1)
     sub = lax.broadcasted_iota(jnp.int32, (8, width), 0)
     wide = lambda x: jnp.broadcast_to(x, (8, width))
@@ -275,7 +276,9 @@
         panel = panels[p]
         base = 8 * p
         cols = [wide(panel[:, base + k : base + k + 1]) for k in range(8)]
-        diag = {(s, k): wide(cols[k][s : s + 1, :]) for k in range(8) for s in range(k, 8)}
+        for k in range(8):
+            scratch[p, k] = cols[k]
+        diag = {(s, k): wide(scratch[p, k, s : s + 1, :]) for k in range(8) for s in range(k, 8)}
         in_block = (lane >= base) & (lane < base + 8)
         mixed = jnp.where(in_block, jnp.where(lane - base == sub, 1.0, 0.0), panel)
         row_a = [wide(panel[s : s + 1, :]) for s in range(8)]
@@ -313,28 +316,35 @@
             back[i] = value * inv[i]
         for q in range(p + 2, count):
             value = jnp.where(in_block, 0.0, panels[q])
-            for k in range(8):
-                value = value - wide(panels[q][:, base + k : base + k + 1]) * back[k]
-            panels[q] = value
+            t = [wide(panels[q][:, base + k : base + k + 1]) * back[k] for k in range(8)]
+            t = ((t[0] + t[1]) + (t[2] + t[3])) + ((t[4] + t[5]) + (t[6] + t[7]))
+            panels[q] = value - t
     return upper, inverse
 
 
-def basis_kernel(scale, gram_ref, state_ref, basis_ref, growth_ref, state, inverse, out, in_sem, out_sem):
+def basis_kernel(scale, gram_ref, state_ref, basis_ref, growth_ref, state, inverse, out, scratch, in_sem, out_sem):
     vectors = gram_ref.shape[0]
     load = pltpu.make_async_copy(state_ref, state, in_sem)
     load.start()
-    upper, low = factor_rows(gram_ref[...], vectors)
+    upper, low = factor_rows(gram_ref[...], vectors, scratch)
     for p, (a, c) in enumerate(zip(upper, low)):
         growth_ref[8 * p : 8 * p + 8, :] = a * (1.0 / scale)
         inverse[8 * p : 8 * p + 8, :] = c * scale
     load.wait()
-    for half in range(2):
-        out[half] = lax.dot_general(
-            state[half], inverse[...], (((1,), (1,)), ((), ())), precision=HIGH, preferred_element_type=jnp.float32
-        )
-        pltpu.make_async_copy(out.at[half], basis_ref.at[half], out_sem.at[half]).start()
-    for half in range(2):
-        pltpu.make_async_copy(out.at[half], basis_ref.at[half], out_sem.at[half]).wait()
+    copies = []
+    for which in range(2):
+        for at in range(0, state.shape[1], state.shape[1] // PIECES):
+            span = pl.ds(at, state.shape[1] // PIECES)
+            out[which, span, :] = lax.dot_general(
+                state[which, span, :], inverse[...], (((1,), (1,)), ((), ())),
+                precision=HIGH, preferred_element_type=jnp.float32,
+            )
+            copies.append(
+                pltpu.make_async_copy(out.at[which, span, :], basis_ref.at[which, span, :], out_sem.at[len(copies)])
+            )
+            copies[-1].start()
+    for copy in copies:
+        copy.wait()
 
 
 def local(tangent, base_v, coupling, columns, *, grid=(4, 4, 2)):
@@ -397,8 +407,9 @@
             pltpu.VMEM((2, rows, vectors), f32),
             pltpu.VMEM((vectors, vectors), f32),
             pltpu.VMEM((2, rows, vectors), f32),
+            pltpu.VMEM((vectors // 8, 8, 8, vectors), f32),
             dma,
-            dma((2,)),
+            dma((2 * PIECES,)),
         ],
         compiler_params=pltpu.CompilerParams(vmem_limit_bytes=40 * 2**20),
     )(gram, state)

time: 69 us -> 67.8 us (0.983)
  Pallas kernels: 68.1 us -> 66.8 us
    pallas_call x1, Pallas kernels: 6.66 us -> 5.48 us  [local(): pl.pallas_call(functools.partial(basis_kernel, scale), out_shape=(jax.Sha...]
where the time goes in v4:
time: 67.8 us; the launch traced here: 67.6 us
  Pallas kernels  66.8 us (99%)
  between operations  0.8 us (1%)
    pallas_call x1, Pallas kernels, local(): pl.pallas_call(functools.partial(tangent_kernel, devices, grid), out_shap...  61.4 us
    pallas_call x1, Pallas kernels, local(): pl.pallas_call(functools.partial(basis_kernel, scale), out_shape=(jax.Sha...  5.48 us

profile of v4, /device:TPU:1, one launch (start us, length us, event | category | flops | bytes accessed | tf_op | source)
XLA Modules:
  0.0 67.6 jit_solution(14670031791649110809)
XLA Ops:
  0.6 61.4 %shard_map.59 = (f32[2,768,128]{2,1,0:T(8,128)S(1)}, f32[128,128]{1,0:T(8,128)S(1)}) custom-call(f32[2,768,128]{2,1,0:T(8,128)} %tan_ref.1, f32[4,768]{1,0:T(4,128)} %v_hbm.1, bf16[3,8,256,256]{3,2,1,0:T(8,128)(2,1)} %coup_ref.1, s32[3,8]{1,0:T(4,128)} %col_hbm.1), custom_call_target="tpu_custom_call" | custom-call | tf_op jit(solution)/shard_map/pallas_call | solution.py:361
  62.0 5.5 %shard_map.60 = (f32[2,768,128]{2,1,0:T(8,128)}, f32[128,128]{1,0:T(8,128)}) custom-call(f32[128,128]{1,0:T(8,128)S(1)} %get-tuple-element.4.gram_ref, f32[2,768,128]{2,1,0:T(8,128)S(1)} %get-tuple-element.5.state_ref), custom_call_target="tpu_custom_call" | custom-call | tf_op jit(solution)/shard_map/pallas_call | solution.py:398

commit v5 on v4

--- a/solution.py
+++ b/solution.py
@@ -176,9 +176,11 @@
         acc[g] += product(pl.ds(0, rows), blocks, operand)
 
     def finish(s, g):
+        operand = []
         for b in range(blocks):
             send(s, g, b, 1).wait_recv()
-        operand = both(*(far[s, g, pl.ds(b * half, half), :] for b in range(blocks)))
+            operand.append(both(far[s, g, pl.ds(b * half, half), :]))
+        operand = jnp.concatenate(operand, axis=0)
         for r in range(blocks):
             span = pl.ds(r * half, half)
             here = pl.ds(r * size, size)
@@ -322,16 +324,17 @@
     return upper, inverse
 
 
-def basis_kernel(scale, gram_ref, state_ref, basis_ref, growth_ref, state, inverse, out, scratch, in_sem, out_sem):
+def basis_kernel(scale, gram_ref, state_ref, basis_ref, growth_ref, state, inverse, out, growth, scratch, in_sem, out_sem):
     vectors = gram_ref.shape[0]
     load = pltpu.make_async_copy(state_ref, state, in_sem)
     load.start()
     upper, low = factor_rows(gram_ref[...], vectors, scratch)
     for p, (a, c) in enumerate(zip(upper, low)):
-        growth_ref[8 * p : 8 * p + 8, :] = a * (1.0 / scale)
+        growth[8 * p : 8 * p + 8, :] = a * (1.0 / scale)
         inverse[8 * p : 8 * p + 8, :] = c * scale
     load.wait()
-    copies = []
+    copies = [pltpu.make_async_copy(growth, growth_ref, out_sem.at[2 * PIECES])]
+    copies[0].start()
     for which in range(2):
         for at in range(0, state.shape[1], state.shape[1] // PIECES):
             span = pl.ds(at, state.shape[1] // PIECES)
@@ -340,7 +343,7 @@
                 precision=HIGH, preferred_element_type=jnp.float32,
             )
             copies.append(
-                pltpu.make_async_copy(out.at[which, span, :], basis_ref.at[which, span, :], out_sem.at[len(copies)])
+                pltpu.make_async_copy(out.at[which, span, :], basis_ref.at[which, span, :], out_sem.at[len(copies) - 1])
             )
             copies[-1].start()
     for copy in copies:
@@ -402,14 +405,15 @@
             jax.ShapeDtypeStruct((vectors, vectors), f32),
         ),
         in_specs=[vmem, anywhere],
-        out_specs=(anywhere, vmem),
+        out_specs=(anywhere, anywhere),
         scratch_shapes=[
             pltpu.VMEM((2, rows, vectors), f32),
             pltpu.VMEM((vectors, vectors), f32),
             pltpu.VMEM((2, rows, vectors), f32),
+            pltpu.VMEM((vectors, vectors), f32),
             pltpu.VMEM((vectors // 8, 8, 8, vectors), f32),
             dma,
-            dma((2 * PIECES,)),
+            dma((2 * PIECES + 1,)),
         ],
         compiler_params=pltpu.CompilerParams(vmem_limit_bytes=40 * 2**20),
     )(gram, state)

time: 67.8 us -> 67 us (0.988)
  Pallas kernels: 66.8 us -> 66.1 us
where the time goes in v5:
time: 67 us; the launch traced here: 66.9 us
  Pallas kernels  66.1 us (99%)
  between operations  0.8 us (1%)
    pallas_call x1, Pallas kernels, local(): pl.pallas_call(functools.partial(tangent_kernel, devices, grid), out_shap...  61.2 us
    pallas_call x1, Pallas kernels, local(): pl.pallas_call(functools.partial(basis_kernel, scale), out_shape=(jax.Sha...  4.87 us

profile of v5, /device:TPU:1, one launch (start us, length us, event | category | flops | bytes accessed | tf_op | source)
XLA Modules:
  0.0 66.9 jit_solution(9119265967109074547)
XLA Ops:
  0.6 61.2 %shard_map.59 = (f32[2,768,128]{2,1,0:T(8,128)S(1)}, f32[128,128]{1,0:T(8,128)S(1)}) custom-call(f32[2,768,128]{2,1,0:T(8,128)} %tan_ref.1, f32[4,768]{1,0:T(4,128)} %v_hbm.1, bf16[3,8,256,256]{3,2,1,0:T(8,128)(2,1)} %coup_ref.1, s32[3,8]{1,0:T(4,128)} %col_hbm.1), custom_call_target="tpu_custom_call" | custom-call | tf_op jit(solution)/shard_map/pallas_call | solution.py:364
  61.8 4.9 %shard_map.60 = (f32[2,768,128]{2,1,0:T(8,128)}, f32[128,128]{1,0:T(8,128)}) custom-call(f32[128,128]{1,0:T(8,128)S(1)} %get-tuple-element.4.gram_ref, f32[2,768,128]{2,1,0:T(8,128)S(1)} %get-tuple-element.5.state_ref), custom_call_target="tpu_custom_call" | custom-call | tf_op jit(solution)/shard_map/pallas_call | solution.py:401
